TPU v7x, 256 devices: a whole 4x4x8 slice. The times are simulated.
256 devices in a mesh: dev: 256 (over z, y, x, core).
Axes of the slice: x: 4, y: 4, z: 8, core: 2. Of those that a mesh axis runs over, the one named last changes fastest.
Arguments:
- features: bfloat16 [262144, 512], P('dev')
- centers: bfloat16 [4096, 512], P('dev')
- target_slot: int32 [262144], P('dev'), may hold values from 0 to 4095
- row_weight: float32 [262144], P('dev'), may hold values from 0.5 to 1.5
Outputs:
- feature_grad: float32 [262144, 512], P('dev')
- center_grad: float32 [4096, 512], P('dev')
All inputs are finite; a program needn't handle non-finite values.
Results may differ from a plain program's by a relative error of at most 0.0051.
Values may be sent and summed in bfloat16 or wider, within the bound.
No kernel may reach another device: no remote copies, remote signals or barrier semaphores. Data moves between devices by JAX's collectives and lax.ppermute only.
A program may use at most 64 MiB of HBM per device.

v0:
```python
import math

import jax
import jax.numpy as jnp
from jax import lax
from jax.sharding import PartitionSpec as P

GROUPS = 2


logit_scale = 64.0
cos_margin = math.cos(0.5)
sin_margin = math.sin(0.5)
sine_offset = 1.01
norm_epsilon = 1e-06


def unit_rows(matrix):
    values = matrix.astype(jnp.float32)
    inverse = lax.rsqrt(jnp.sum(values * values, axis=1, keepdims=True) + norm_epsilon)
    return (inverse, values * inverse)


def project_back(inverse, unit, gradient):
    return inverse * (gradient - unit * jnp.sum(gradient * unit, axis=1, keepdims=True))


def shifted_exp(cosine, is_target):
    sines = jnp.sqrt(sine_offset - cosine * cosine)
    target_logit = logit_scale * (cosine * cos_margin - sines * sin_margin)
    logits = jnp.where(is_target, target_logit, logit_scale * cosine)
    return jnp.exp(logits - logit_scale)


def cosine_grad(cosine, is_target, exponent, totals, weights):
    sines = jnp.sqrt(sine_offset - cosine * cosine)
    onehot = is_target.astype(jnp.float32)
    logit_grad = weights[:, None] * (exponent / totals[:, None] - onehot)
    slopes = jnp.where(is_target, cos_margin + cosine * sin_margin / sines, 1.0)
    return (logit_scale * logit_grad * slopes).astype(jnp.bfloat16)


def center_term(grads, rows_in):
    return lax.dot_general(
        grads, rows_in, (((0,), (0,)), ((), ())), preferred_element_type=jnp.float32
    )


def per_device(features, centers, target_slot, row_weight):
    rows_dev = features.shape[0]
    center_count = centers.shape[0]
    group_rows = rows_dev // GROUPS
    inv_f, unit_f = unit_rows(features)
    normed_f = unit_f.astype(jnp.bfloat16)
    inv_c, unit_c = unit_rows(centers)
    normed_c = unit_c.astype(jnp.bfloat16)
    gathered = lax.all_gather(normed_c, "dev", axis=0, tiled=True)
    column_ids = jnp.arange(gathered.shape[0], dtype=jnp.int32)
    row_parts = []
    grad_parts = []
    center_sum = jnp.zeros((center_count, features.shape[1]), jnp.float32)
    for group in range(GROUPS):
        lower = group * group_rows
        rows_in = normed_f[lower : lower + group_rows]
        cosine = jnp.dot(rows_in, gathered.T, preferred_element_type=jnp.float32)
        is_target = column_ids[None, :] == target_slot[lower : lower + group_rows][:, None]
        exponent = shifted_exp(cosine, is_target)
        totals = jnp.sum(exponent, axis=1)
        grads = cosine_grad(
            cosine, is_target, exponent, totals, row_weight[lower : lower + group_rows]
        )
        row_parts.append(jnp.dot(grads, gathered, preferred_element_type=jnp.float32))
        grad_parts.append(grads)
        center_sum = center_sum + lax.psum_scatter(
            center_term(grads, rows_in), "dev", scatter_dimension=0, tiled=True
        )
    row_sum = jnp.concatenate(row_parts, axis=0)
    return (project_back(inv_f, unit_f, row_sum), project_back(inv_c, unit_c, center_sum))


def solution(mesh):
    return jax.shard_map(
        per_device,
        mesh=mesh,
        in_specs=(P("dev", None), P("dev", None), P("dev"), P("dev")),
        out_specs=(P("dev", None), P("dev", None)),
        check_vma=False,
    )
```

profile of v0, /device:TPU:2, one launch (start us, length us, event | category | flops | bytes accessed | tf_op | source)
XLA Modules:
  0.0 1454.4 jit_solution(12000695746708671085)
XLA Ops:
  7.2 0.0 all-gather.2.cloned.1.call-start
  7.2 0.8 fusion.22
  8.1 1.4 fusion.18
  9.5 0.0 all-gather.2.cloned.1.call-update
  9.5 0.0 reduce-scatter.2.cloned.1.call-start
  9.5 1.5 fusion.8
  11.0 0.8 fusion.24
  11.8 0.8 fusion.23
  12.6 1.5 fusion.4
  14.1 116.2 %all-gather.2.cloned.1.call-done = bf16[4096,512]{1,0:T(8,128)(2,1)} async-done(((bf16[16,512]{1,0:T(8,128)(2,1)}), bf16[4096,512]{1,0:T(8,128)(2,1)}) %all-gather.2.cloned.1.call-update) | async-done | bytes 4194320 | tf_op jit(solution)/shard_map/all_gather | solution.py:57
  130.3 9.1 fusion.1
  139.4 7.0 fusion
  146.3 17.8 %multiply_convert_fusion = (bf16[512,4096]{1,0:T(8,128)(2,1)S(1)}, bf16[512,4096]{1,0:T(8,128)(2,1)S(1)}) fusion(f32[512,4096]{1,0:T(8,128)S(1)} %get-tuple-element.7, f32[512]{0:T(512)S(1)} %get-tuple-element.6, s32[512]{0:T(512)S(1)} %get-tuple-element.5, f32[512]{0:T(512)S(1)} %get-tuple-element.3, f32[512,4096]{1,0:T(8,128)S(1)} %get-tuple-element.9, ...), kind=kLoop, calls=%fused_computation | loop fusion | flops 88080384 | bytes 25178112 | tf_op jit(solution)/shard_map/convert_element_type | solution.py:40
  164.1 1.9 copy-done.1
  166.1 2.4 fusion.12
  168.5 5.8 convolution_add_fusion
  174.3 0.0 reduce-scatter.2.cloned.1.call-update
  174.4 5.9 fusion.26
  180.3 2.3 fusion.25
  182.7 0.6 fusion.5
  183.2 1.7 fusion.7
  185.0 1260.2 %reduce-scatter.2.cloned.1.call-done = f32[16,512]{1,0:T(8,128)} async-done(((f32[4096,512]{1,0:T(8,128)}), f32[16,512]{1,0:T(8,128)}) %reduce-scatter.2.cloned.1.call-update) | async-done | bytes 32784 | tf_op jit(solution)/shard_map/reduce_scatter | solution.py:74
  1445.2 0.9 fusion.19
  1446.1 1.5 fusion.21
  (15 shorter events, 0.0 us)
Async XLA Ops:
  7.2 123.1 %all-gather.2.cloned.1.call-start = ((), (), s32[]{:S(2)}) async-start(), calls=%async_computation.1 | async-start | bytes 4210688 | tf_op jit(solution)/shard_map/all_gather | solution.py:57
  9.5 1435.7 %reduce-scatter.2.cloned.1.call-start = ((), (), s32[]{:S(2)}) async-start(), calls=%async_computation.2 | async-start | bytes 8421376 | tf_op jit(solution)/shard_map/reduce_scatter | solution.py:74
  130.3 9.1 copy-start.5
  164.1 2.0 copy-start.1
  164.1 4.3 copy-start
  174.3 5.9 copy-start.2
  174.4 5.9 copy-start.6
  180.3 2.3 copy-start.3
  182.7 1262.5 %copy-start.4 = (bf16[16,512]{1,0:T(8,128)(2,1)S(1)}, bf16[16,512]{1,0:T(8,128)(2,1)}, u32[]{:S(2)}) copy-start(bf16[16,512]{1,0:T(8,128)(2,1)} %param.5) | copy-start | bytes 49156
Sparse Core Ops, SparseCore 0:
  12.2 118.0 all-gather.1
  174.5 1270.6 reduce-scatter.1
where the time goes:
time: 1460 us; the launch traced here: 1450 us
  waiting for transfers between devices  1380 us (95%)
  matrix products  32.5 us (2%)
  other arithmetic  27.7 us (2%)
    reduce_scatter x1, waiting for transfers between devices, per_device(): lax.psum_scatter(center_term(grads, rows_in), 'dev', scatter_dimension=0,...  1260 us
    all_gather x1, waiting for transfers between devices, per_device(): gathered = lax.all_gather(normed_c, 'dev', axis=0, tiled=True)  116 us
  transfers between devices with their start and end apart: 2, of which 2 were waited for; matrix products, arithmetic and copies ran while one was open for 1% of the time, Pallas kernels for 0%

commit v1 on v0

v1 whole, which is shorter than its diff:
```python
import math

import jax
import jax.numpy as jnp
from jax import lax
from jax.experimental import pallas as pl
from jax.experimental.pallas import tpu as pltpu
from jax.sharding import PartitionSpec as P

SIDE_Z, SIDE_Y, SIDE_X, CORES = 8, 4, 4, 2
DEVICES = SIDE_Z * SIDE_Y * SIDE_X * CORES
LINE = 4
TILE = 512
VMEM_LIMIT = 32 * 1024 * 1024

logit_scale = 64.0
cos_margin = math.cos(0.5)
sin_margin = math.sin(0.5)
sine_offset = 1.01
norm_epsilon = 1e-06
log2_e = math.log2(math.e)
scale2 = logit_scale * log2_e


def device_of(z, y, x, core):
    return ((z * SIDE_Y + y) * SIDE_X + x) * CORES + core


def coordinates(device):
    core = device % CORES
    x = device // CORES % SIDE_X
    y = device // (CORES * SIDE_X) % SIDE_Y
    z = device // (CORES * SIDE_X * SIDE_Y)
    return z, y, x, core


def core_pairs():
    return [(d, d ^ 1) for d in range(DEVICES)]


def line_shift(step):
    pairs = []
    for d in range(DEVICES):
        z, y, x, core = coordinates(d)
        if core == 0:
            pairs.append((d, device_of(z, y, (x + step) % LINE, core)))
        else:
            pairs.append((d, device_of(z, (y + step) % LINE, x, core)))
    return pairs


def plane_groups():
    groups = []
    for fixed in range(LINE):
        groups.append([device_of(z, u, fixed, 0) for z in range(SIDE_Z) for u in range(LINE)])
        groups.append([device_of(z, fixed, u, 1) for z in range(SIDE_Z) for u in range(LINE)])
    return groups


def call(kernel, outs, name, flops=0, moved=0):
    return pl.pallas_call(
        kernel,
        out_shape=outs,
        compiler_params=pltpu.CompilerParams(vmem_limit_bytes=VMEM_LIMIT),
        cost_estimate=pl.CostEstimate(flops=flops, bytes_accessed=moved, transcendentals=0),
        name=name,
    )


def unit_rows(matrix):
    values = matrix.astype(jnp.float32)
    inverse = lax.rsqrt(jnp.sum(values * values, axis=1, keepdims=True) + norm_epsilon)
    return inverse, values * inverse


def project_back(inverse, unit, gradient):
    return inverse * (gradient - unit * jnp.sum(gradient * unit, axis=1, keepdims=True))


def prepare_kernel(own_ref, other_ref, normed_ref, turned_ref):
    half = own_ref.shape[0]
    for part, ref in enumerate((own_ref, other_ref)):
        for low in range(0, half, 256):
            _, unit = unit_rows(ref[low : low + 256, :])
            rows = slice(part * half + low, part * half + low + 256)
            normed_ref[rows, :] = unit.astype(jnp.bfloat16)
            turned_ref[:, rows] = unit.T.astype(jnp.bfloat16)


def totals_kernel(chunk, first, *refs):
    if first:
        centers_ref, turned_ref, place_ref, out_ref = refs
    else:
        centers_ref, turned_ref, place_ref, before_ref, out_ref = refs
    count = centers_ref.shape[0]
    rows = turned_ref.shape[1]
    ids = lax.broadcasted_iota(jnp.int32, (count, TILE), 0) + chunk * count
    for low in range(0, rows, TILE):
        lanes = slice(low, low + TILE)
        cosine = jnp.dot(centers_ref[...], turned_ref[:, lanes], preferred_element_type=jnp.float32)
        is_target = ids == place_ref[:, lanes]
        exponent = jnp.where(is_target, 0.0, jnp.exp2(cosine * scale2 - scale2))
        total = jnp.sum(exponent, axis=0, keepdims=True)
        target = jnp.sum(jnp.where(is_target, cosine, 0.0), axis=0, keepdims=True)
        if not first:
            total = total + before_ref[0:1, lanes]
            target = target + before_ref[1:2, lanes]
        out_ref[0:1, lanes] = total
        out_ref[1:2, lanes] = target


def grads_kernel(chunk, centers_ref, normed_ref, turned_ref, place_ref, mine_ref, other_ref, weight_ref, grads_ref, term_ref):
    count = centers_ref.shape[0]
    rows = turned_ref.shape[1]
    half = rows // 2
    ids = lax.broadcasted_iota(jnp.int32, (count, TILE), 0) + chunk * count
    term = jnp.zeros(term_ref.shape, jnp.float32)
    for low in range(0, rows, TILE):
        lanes = slice(low, low + TILE)
        there = (low + half) % rows
        both = mine_ref[:, lanes] + other_ref[:, there : there + TILE]
        partial, target = both[0:1], both[1:2]
        weight = logit_scale * weight_ref[:, lanes]
        sines = jnp.sqrt(sine_offset - target * target)
        logit = logit_scale * (target * cos_margin - sines * sin_margin)
        at_target = jnp.exp(logit - logit_scale)
        total = partial + at_target
        slope = cos_margin + target * sin_margin / sines
        target_grad = weight * (at_target / total - 1.0) * slope
        shift = (jnp.log(weight) - jnp.log(total)) * log2_e - scale2
        cosine = jnp.dot(centers_ref[...], turned_ref[:, lanes], preferred_element_type=jnp.float32)
        grads = jnp.exp2(cosine * scale2 + shift)
        grads = jnp.where(ids == place_ref[:, lanes], target_grad, grads).astype(jnp.bfloat16)
        grads_ref[:, lanes] = grads
        term = term + jnp.dot(grads, normed_ref[lanes, :], preferred_element_type=jnp.float32)
    term_ref[...] = term.astype(term_ref.dtype)


def rows_kernel(half, *refs):
    centers_refs, grads_refs, out_ref = refs[:LINE], refs[LINE : 2 * LINE], refs[2 * LINE]
    count = out_ref.shape[1]
    turned = [ref[...].T for ref in centers_refs]
    for low in range(0, count, TILE):
        lanes = slice(half * count + low, half * count + low + TILE)
        total = jnp.zeros((out_ref.shape[0], TILE), jnp.float32)
        for center, ref in zip(turned, grads_refs):
            total = total + jnp.dot(center, ref[:, lanes], preferred_element_type=jnp.float32)
        out_ref[:, low : low + TILE] = total.astype(out_ref.dtype)


def feature_kernel(features_ref, mine_ref, other_ref, out_ref):
    for low in range(0, out_ref.shape[0], 256):
        rows = slice(low, low + 256)
        inverse, unit = unit_rows(features_ref[rows, :])
        gradient = (mine_ref[:, rows] + other_ref[:, rows].astype(jnp.float32)).T
        out_ref[rows, :] = project_back(inverse, unit, gradient)


def center_kernel(centers_ref, terms_ref, out_ref):
    inverse, unit = unit_rows(centers_ref[...])
    gradient = terms_ref[0].astype(jnp.float32)
    for peer in range(1, terms_ref.shape[0]):
        gradient = gradient + terms_ref[peer].astype(jnp.float32)
    out_ref[...] = project_back(inverse, unit, gradient)


def sum_kernel(own_ref, *refs):
    out_ref = refs[-1]
    total = own_ref[...].astype(jnp.float32)
    for ref in refs[:-1]:
        total = total + ref[...].astype(jnp.float32)
    out_ref[...] = total.astype(out_ref.dtype)


def per_device(features, centers, target_slot, row_weight):
    rows_dev, width = features.shape
    own_centers = centers.shape[0]
    rows = CORES * rows_dev
    count = own_centers * SIDE_Z * LINE
    groups = plane_groups()
    peers = len(groups[0])
    z, y, x, core = coordinates(lax.axis_index("dev"))

    _, unit_c = unit_rows(centers)
    normed_c = unit_c.astype(jnp.bfloat16)
    own_chunk = lax.all_to_all(
        jnp.broadcast_to(normed_c[None], (peers, own_centers, width)),
        "dev", 0, 0, axis_index_groups=groups, tiled=True,
    ).reshape(count, width)
    chunks = [own_chunk] + [lax.ppermute(own_chunk, "dev", line_shift(k)) for k in range(1, LINE)]

    features_other = lax.ppermute(features, "dev", core_pairs())
    slot_other = lax.ppermute(target_slot, "dev", core_pairs())
    weight_other = lax.ppermute(row_weight, "dev", core_pairs())
    weight = jnp.concatenate([row_weight, weight_other]).reshape(1, rows)
    slot = jnp.concatenate([target_slot, slot_other])
    slot_z, slot_y, slot_x, slot_core = coordinates(slot // own_centers)
    across = jnp.where(core == 0, slot_y, slot_x)
    along = jnp.where(core == 0, x - slot_x, y - slot_y) % LINE
    place = along * count + (slot_z * LINE + across) * own_centers + slot % own_centers
    place = jnp.where(slot_core == core, place, -1).reshape(1, rows)

    normed_f, turned_f = call(
        prepare_kernel,
        (jax.ShapeDtypeStruct((rows, width), jnp.bfloat16), jax.ShapeDtypeStruct((width, rows), jnp.bfloat16)),
        "prepare", 0, 6 * rows * width,
    )(features, features_other)

    work = 2 * count * rows * width
    mine = None
    for chunk in (0, 1, 3, 2):
        before = () if mine is None else (mine,)
        mine = call(
            lambda *refs, chunk=chunk, first=mine is None: totals_kernel(chunk, first, *refs),
            jax.ShapeDtypeStruct((2, rows), jnp.float32), "totals%d" % chunk, work, 0,
        )(chunks[chunk], turned_f, place, *before)
    other = lax.ppermute(mine, "dev", core_pairs())

    grads, terms = [None] * LINE, [None] * LINE
    for chunk in (2, 1, 3, 0):
        grads[chunk], terms[chunk] = call(
            lambda *refs, chunk=chunk: grads_kernel(chunk, *refs),
            (jax.ShapeDtypeStruct((count, rows), jnp.bfloat16), jax.ShapeDtypeStruct((count, width), jnp.bfloat16)),
            "grads%d" % chunk, 2 * work, 0,
        )(chunks[chunk], normed_f, turned_f, place, mine, other, weight)
        if chunk:
            terms[chunk] = lax.ppermute(terms[chunk], "dev", line_shift(-chunk))

    row_other = call(
        lambda *refs: rows_kernel(1, *refs), jax.ShapeDtypeStruct((width, rows_dev), jnp.bfloat16), "rows_other", 2 * work, 0,
    )(*chunks, *grads)
    row_other = lax.ppermute(row_other, "dev", core_pairs())
    row_mine = call(
        lambda *refs: rows_kernel(0, *refs), jax.ShapeDtypeStruct((width, rows_dev), jnp.float32), "rows_mine", 2 * work, 0,
    )(*chunks, *grads)
    feature_grad = call(
        feature_kernel, jax.ShapeDtypeStruct((rows_dev, width), jnp.float32), "feature_grad", 0, 8 * rows_dev * width,
    )(features, row_mine, row_other)

    line_sum = call(sum_kernel, jax.ShapeDtypeStruct((count, width), jnp.bfloat16), "line_sum", 0, 10 * count * width)(*terms)
    plane = lax.all_to_all(
        line_sum.reshape(peers, own_centers, width), "dev", 0, 0, axis_index_groups=groups, tiled=True
    )
    center_grad = call(
        center_kernel, jax.ShapeDtypeStruct((own_centers, width), jnp.float32), "center_grad", 0, 2 * count * width,
    )(centers, plane)
    return feature_grad, center_grad


def solution(mesh):
    return jax.shard_map(
        per_device,
        mesh=mesh,
        in_specs=(P("dev", None), P("dev", None), P("dev"), P("dev")),
        out_specs=(P("dev", None), P("dev", None)),
        check_vma=False,
    )
```

time: 1460 us -> 104 us (0.07)
  waiting for transfers between devices: 1380 us -> 30.8 us
  matrix products: 32.5 us -> 0 us
  Pallas kernels: 0 us -> 31.2 us
  starting transfers between devices: 0.08 us -> 27.5 us
  other arithmetic: 27.7 us -> 2.68 us
    reduce_scatter x1 -> x0, waiting for transfers between devices: 1260 us -> none  [per_device(): lax.psum_scatter(center_term(grads, rows_in), 'dev', scatter_dimension=0,...]
    all_gather x1 -> x0, waiting for transfers between devices: 116 us -> none  [per_device(): gathered = lax.all_gather(normed_c, 'dev', axis=0, tiled=True)]
    dot_general x6 -> x0, matrix products: 32.5 us -> none  [the longest x2 16 us: per_device(): cosine = jnp.dot(rows_in, gathered.T, preferred_element_type=jnp.float32)]
    pallas_call x0 -> x14, Pallas kernels: none -> 31.2 us  [the longest x4 9.61 us: per_device(): call(lambda *refs, chunk=chunk: grads_kernel(chunk, *refs), (jax.ShapeDty...]
    all_to_all x0 -> x2, waiting for transfers between devices: none -> 21.1 us  [the longest x1 17.7 us: per_device(): lax.all_to_all(jnp.broadcast_to(normed_c[None], (peers, own_centers, widt...]
    convert_element_type x2 -> x0, other arithmetic: 19.3 us -> none  [the longest x1 17.8 us: cosine_grad(): return (logit_scale * logit_grad * slopes).astype(jnp.bfloat16)]
    all_to_all x0 -> x2, starting transfers between devices: none -> 16.4 us  [the longest x1 11.5 us: per_device(): lax.all_to_all(jnp.broadcast_to(normed_c[None], (peers, own_centers, widt...]
  transfers between devices with their start and end apart: 2 -> 13, of which waited for: 2 -> 6; matrix products, arithmetic and copies ran while one was open for 1% -> 1% of each run, Pallas kernels for 0% -> 26%
where the time goes in v1:
time: 104 us; the launch traced here: 103 us
  Pallas kernels  31.2 us (30%)
  waiting for transfers between devices  30.8 us (30%)
  starting transfers between devices  27.5 us (26%)
  local copies, waits for them, and re-layouts  9.63 us (9%)
  other arithmetic  2.68 us (3%)
    all_to_all x1, waiting for transfers between devices, per_device(): lax.all_to_all(jnp.broadcast_to(normed_c[None], (peers, own_centers, widt...  17.7 us
    all_to_all x1, starting transfers between devices, per_device(): lax.all_to_all(jnp.broadcast_to(normed_c[None], (peers, own_centers, widt...  11.5 us
    pallas_call x4, Pallas kernels, per_device(): call(lambda *refs, chunk=chunk: grads_kernel(chunk, *refs), (jax.ShapeDty...  9.61 us
    unnamed x34, local copies, waits for them, and re-layouts  8.78 us
    pallas_call x4, Pallas kernels, per_device(): call(lambda *refs, chunk=chunk, first=mine is None: totals_kernel(chunk,...  7.59 us
    ppermute x3, starting transfers between devices, per_device(): terms[chunk] = lax.ppermute(terms[chunk], 'dev', line_shift(-chunk))  6.26 us
    all_to_all x1, starting transfers between devices, per_device(): lax.all_to_all(line_sum.reshape(peers, own_centers, width), 'dev', 0, 0,...  4.88 us
    ppermute x3, waiting for transfers between devices, per_device(): terms[chunk] = lax.ppermute(terms[chunk], 'dev', line_shift(-chunk))  4.53 us
  transfers between devices with their start and end apart: 13, of which 6 were waited for; matrix products, arithmetic and copies ran while one was open for 1% of the time, Pallas kernels for 26%

profile of v1, /device:TPU:2, one launch (start us, length us, event | category | flops | bytes accessed | tf_op | source)
XLA Modules:
  0.0 102.8 jit_solution(18042000722434369793)
XLA Ops:
  3.2 11.5 %all-to-all-start = ((bf16[32,16,512]{2,1,0:T(8,128)(2,1)}), bf16[32,16,512]{2,1,0:T(8,128)(2,1)S(1)}, u32[]{:S(2)}, u32[]{:S(2)}) async-start(bf16[32,16,512]{2,1,0:T(8,128)(2,1)} %broadcast_in_dim.3), calls=%async_computation | async-start | bytes 1048576 | tf_op jit(solution)/shard_map/all_to_all | solution.py:186
  14.8 17.7 %all-to-all-done = bf16[32,16,512]{2,1,0:T(8,128)(2,1)S(1)} async-done(((bf16[32,16,512]{2,1,0:T(8,128)(2,1)}), bf16[32,16,512]{2,1,0:T(8,128)(2,1)S(1)}, u32[]{:S(2)}, u32[]{:S(2)}) %all-to-all-start) | async-done | bytes 524320 | tf_op jit(solution)/shard_map/all_to_all | solution.py:186
  32.5 1.8 %collective-permute-start = (bf16[512,512]{1,0:T(8,128)(2,1)S(1)}, bf16[512,512]{1,0:T(8,128)(2,1)S(1)}, u32[]{:S(2)}, u32[]{:S(2)}) collective-permute-start(bf16[512,512]{1,0:T(8,128)(2,1)S(1)} %bitcast.5), channel_id=1, source_target_pairs={{0,2},{1,9},{2,4},{3,11},{4,6},{5,13},{6,0},{7,15},{8,10},{9,17},{... | collective-permute-start | bytes 1572872 | tf_op jit(solution)/shard_map/ppermute | solution.py:190
  36.0 2.1 %collective-permute-start.1 = (bf16[512,512]{1,0:T(8,128)(2,1)S(1)}, bf16[512,512]{1,0:T(8,128)(2,1)S(1)}, u32[]{:S(2)}, u32[]{:S(2)}) collective-permute-start(bf16[512,512]{1,0:T(8,128)(2,1)S(1)} %bitcast.7), channel_id=1, source_target_pairs={{0,4},{1,17},{2,6},{3,19},{4,0},{5,21},{6,2},{7,23},{8,12},{9,25},... | collective-permute-start | bytes 1572872 | tf_op jit(solution)/shard_map/ppermute | solution.py:190
  39.1 2.4 %prepare.1 = (bf16[2048,512]{1,0:T(8,128)(2,1)S(1)}, bf16[512,2048]{1,0:T(8,128)(2,1)S(1)}) custom-call(bf16[1024,512]{1,0:T(8,128)(2,1)S(1)} %copy-done.6, bf16[1024,512]{1,0:T(8,128)(2,1)} %collective-permute-done.3.other_ref), custom_call_target="tpu_custom_call" | custom-call | bytes 6291456 | tf_op jit(solution)/shard_map/prepare/pallas_call | solution.py:203
  41.5 2.0 %totals0.1.refs_3_ = f32[2,2048]{1,0:T(2,128)S(1)} custom-call(bf16[512,512]{1,0:T(8,128)(2,1)S(1)} %bitcast.8, bf16[512,2048]{1,0:T(8,128)(2,1)S(1)} %get-tuple-element.13.refs_1_.refs_2_, s32[1,2048]{1,0:T(1,128)S(1)} %compare_select_fusion.6.refs_2_.refs_3_), custom_call_target="tpu_custom_call" | custom-call | flops 1073741824 | tf_op jit(solution)/shard_map/totals0/pallas_call | solution.py:213
  43.4 3.2 %collective-permute-done.refs_0_.refs_1_ = bf16[512,512]{1,0:T(8,128)(2,1)S(1)} collective-permute-done((bf16[512,512]{1,0:T(8,128)(2,1)S(1)}, bf16[512,512]{1,0:T(8,128)(2,1)S(1)}, u32[]{:S(2)}, u32[]{:S(2)}) %collective-permute-start) | collective-permute-done | bytes 524320 | tf_op jit(solution)/shard_map/ppermute | solution.py:190
  46.7 1.9 %totals1.1.refs_3_ = f32[2,2048]{1,0:T(2,128)S(1)} custom-call(bf16[512,512]{1,0:T(8,128)(2,1)S(1)} %collective-permute-done.refs_0_.refs_1_, bf16[512,2048]{1,0:T(8,128)(2,1)S(1)} %get-tuple-element.13.refs_1_.refs_2_, s32[1,2048]{1,0:T(1,128)S(1)} %compare_select_fusion.6.refs_2_.refs_3_, f32[2,2048]{1,0:T(2,128)S(1)} %totals0.1.refs_3_), custom_call_target="tpu_custom_call" | custom-call | flops 1073741824 | tf_op jit(solution)/shard_map/totals1/pallas_call | solution.py:213
  48.6 1.9 %totals3.1.refs_3_ = f32[2,2048]{1,0:T(2,128)S(1)} custom-call(bf16[512,512]{1,0:T(8,128)(2,1)S(1)} %collective-permute-done.2.refs_0_.refs_3_, bf16[512,2048]{1,0:T(8,128)(2,1)S(1)} %get-tuple-element.13.refs_1_.refs_2_, s32[1,2048]{1,0:T(1,128)S(1)} %compare_select_fusion.6.refs_2_.refs_3_, f32[2,2048]{1,0:T(2,128)S(1)} %totals1.1.refs_3_), custom_call_target="tpu_custom_call" | custom-call | flops 1073741824 | tf_op jit(solution)/shard_map/totals3/pallas_call | solution.py:213
  50.5 1.9 %totals2.1.refs_4_ = f32[2,2048]{1,0:T(2,128)S(1)} custom-call(bf16[512,512]{1,0:T(8,128)(2,1)S(1)} %collective-permute-done.1.refs_0_.refs_2_, bf16[512,2048]{1,0:T(8,128)(2,1)S(1)} %get-tuple-element.13.refs_1_.refs_2_, s32[1,2048]{1,0:T(1,128)S(1)} %compare_select_fusion.6.refs_2_.refs_3_, f32[2,2048]{1,0:T(2,128)S(1)} %totals3.1.refs_3_), custom_call_target="tpu_custom_call" | custom-call | flops 1073741824 | tf_op jit(solution)/shard_map/totals2/pallas_call | solution.py:213
  54.7 2.4 %grads3.1 = (bf16[512,2048]{1,0:T(8,128)(2,1)S(1)}, bf16[512,512]{1,0:T(8,128)(2,1)S(1)}) custom-call(bf16[512,512]{1,0:T(8,128)(2,1)S(1)} %copy-done.9, bf16[2048,512]{1,0:T(8,128)(2,1)S(1)} %get-tuple-element.12.refs_1_, bf16[512,2048]{1,0:T(8,128)(2,1)S(1)} %get-tuple-element.13.refs_1_.refs_2_, s32[1,2048]{1,0:T(1,128)S(1)} %compare_select_fusion.6.refs_2_.refs_3_, ...), custom_call_target="tpu_custom_call" | custom-call | flops 2147483648 | tf_op jit(solution)/shard_map/grads3/pallas_call | solution.py:221
  57.0 2.7 %collective-permute-start.10 = (bf16[512,512]{1,0:T(8,128)(2,1)S(1)}, bf16[512,512]{1,0:T(8,128)(2,1)S(1)}, u32[]{:S(2)}, u32[]{:S(2)}) collective-permute-start(bf16[512,512]{1,0:T(8,128)(2,1)S(1)} %get-tuple-element.21), channel_id=1, source_target_pairs={{0,2},{1,9},{2,4},{3,11},{4,6},{5,13},{6,0},{7,15},{8,10},{9,17},{... | collective-permute-start | bytes 1572872 | tf_op jit(solution)/shard_map/ppermute | solution.py:227
  59.8 2.4 %grads2.1 = (bf16[512,2048]{1,0:T(8,128)(2,1)S(1)}, bf16[512,512]{1,0:T(8,128)(2,1)S(1)}) custom-call(bf16[512,512]{1,0:T(8,128)(2,1)S(1)} %collective-permute-done.1.refs_0_.refs_2_, bf16[2048,512]{1,0:T(8,128)(2,1)S(1)} %get-tuple-element.12.refs_1_, bf16[512,2048]{1,0:T(8,128)(2,1)S(1)} %get-tuple-element.13.refs_1_.refs_2_, ...), custom_call_target="tpu_custom_call" | custom-call | flops 2147483648 | tf_op jit(solution)/shard_map/grads2/pallas_call | solution.py:221
  63.0 2.4 %grads1.1 = (bf16[512,2048]{1,0:T(8,128)(2,1)S(1)}, bf16[512,512]{1,0:T(8,128)(2,1)S(1)}) custom-call(bf16[512,512]{1,0:T(8,128)(2,1)S(1)} %collective-permute-done.refs_0_.refs_1_, bf16[2048,512]{1,0:T(8,128)(2,1)S(1)} %get-tuple-element.12.refs_1_, bf16[512,2048]{1,0:T(8,128)(2,1)S(1)} %get-tuple-element.13.refs_1_.refs_2_, ...), custom_call_target="tpu_custom_call" | custom-call | flops 2147483648 | tf_op jit(solution)/shard_map/grads1/pallas_call | solution.py:221
  65.4 2.7 %collective-permute-start.8 = (bf16[512,512]{1,0:T(8,128)(2,1)S(1)}, bf16[512,512]{1,0:T(8,128)(2,1)S(1)}, u32[]{:S(2)}, u32[]{:S(2)}) collective-permute-start(bf16[512,512]{1,0:T(8,128)(2,1)S(1)} %get-tuple-element.19), channel_id=1, source_target_pairs={{0,6},{1,25},{2,0},{3,27},{4,2},{5,29},{6,4},{7,31},{8,14},{9,1},{... | collective-permute-start | bytes 1572872 | tf_op jit(solution)/shard_map/ppermute | solution.py:227
  68.1 2.5 %grads0.1 = (bf16[512,2048]{1,0:T(8,128)(2,1)S(1)}, bf16[512,512]{1,0:T(8,128)(2,1)S(1)}) custom-call(bf16[512,512]{1,0:T(8,128)(2,1)S(1)} %bitcast.9, bf16[2048,512]{1,0:T(8,128)(2,1)S(1)} %get-tuple-element.12.refs_1_, bf16[512,2048]{1,0:T(8,128)(2,1)S(1)} %get-tuple-element.13.refs_1_.refs_2_, s32[1,2048]{1,0:T(1,128)S(1)} %compare_select_fusion.6.refs_2_.refs_3_, ...), custom_call_target="tpu_custom_call" | custom-call | flops 2147483648 | tf_op jit(solution)/shard_map/grads0/pallas_call | solution.py:221
  70.6 3.4 %rows_other.1 = bf16[512,1024]{1,0:T(8,128)(2,1)} custom-call(bf16[512,512]{1,0:T(8,128)(2,1)S(1)} %bitcast.10, bf16[512,512]{1,0:T(8,128)(2,1)S(1)} %collective-permute-done.refs_0_.refs_1_, bf16[512,512]{1,0:T(8,128)(2,1)S(1)} %collective-permute-done.1.refs_0_.refs_2_, bf16[512,512]{1,0:T(8,128)(2,1)S(1)} %copy-done.10, ...), custom_call_target="tpu_custom_call" | custom-call | flops 2147483648 | tf_op jit(solution)/shard_map/rows_other/pallas_call | solution.py:229
  74.1 4.5 %collective-permute-done.8.refs_0_ = bf16[512,512]{1,0:T(8,128)(2,1)S(1)} collective-permute-done((bf16[512,512]{1,0:T(8,128)(2,1)S(1)}, bf16[512,512]{1,0:T(8,128)(2,1)S(1)}, u32[]{:S(2)}, u32[]{:S(2)}) %collective-permute-start.8) | collective-permute-done | bytes 524320 | tf_op jit(solution)/shard_map/ppermute | solution.py:227
  79.7 4.9 %all-to-all-start.1 = ((bf16[32,16,512]{2,1,0:T(8,128)(2,1)}), bf16[32,16,512]{2,1,0:T(8,128)(2,1)}, u32[]{:S(2)}, u32[]{:S(2)}) async-start(bf16[32,16,512]{2,1,0:T(8,128)(2,1)} %bitcast.12), calls=%async_computation.1 | async-start | bytes 1048576 | tf_op jit(solution)/shard_map/all_to_all | solution.py:241
  87.8 1.6 %copy-done.5 = bf16[512,2048]{1,0:T(8,128)(2,1)S(1)} copy-done((bf16[512,2048]{1,0:T(8,128)(2,1)S(1)}, bf16[512,2048]{1,0:T(8,128)(2,1)}, u32[]{:S(2)}) %copy-start.5) | copy-done | bytes 2097176
  91.4 2.4 %rows_mine.1.mine_ref = f32[512,1024]{1,0:T(8,128)S(1)} custom-call(bf16[512,512]{1,0:T(8,128)(2,1)S(1)} %bitcast.11, bf16[512,512]{1,0:T(8,128)(2,1)S(1)} %collective-permute-done.refs_0_.refs_1_, bf16[512,512]{1,0:T(8,128)(2,1)S(1)} %copy-done.13, bf16[512,512]{1,0:T(8,128)(2,1)S(1)} %copy-done.11, bf16[512,2048]{1,0:T(8,128)(2,1)S(1)} %copy-done.5, ...), custom_call_target="tpu_custom_call" | custom-call | flops 2147483648 | tf_op jit(solution)/shard_map/rows_mine/pallas_call | solution.py:233
  93.8 3.8 %feature_grad.1 = f32[1024,512]{1,0:T(8,128)} custom-call(bf16[1024,512]{1,0:T(8,128)(2,1)S(1)} %copy-done.7, f32[512,1024]{1,0:T(8,128)S(1)} %rows_mine.1.mine_ref, bf16[512,1024]{1,0:T(8,128)(2,1)} %collective-permute-done.7.other_ref), custom_call_target="tpu_custom_call" | custom-call | bytes 4194304 | tf_op jit(solution)/shard_map/feature_grad/pallas_call | solution.py:236
  97.6 3.4 %all-to-all-done.1.terms_ref = bf16[32,16,512]{2,1,0:T(8,128)(2,1)} async-done(((bf16[32,16,512]{2,1,0:T(8,128)(2,1)}), bf16[32,16,512]{2,1,0:T(8,128)(2,1)}, u32[]{:S(2)}, u32[]{:S(2)}) %all-to-all-start.1) | async-done | bytes 524320 | tf_op jit(solution)/shard_map/all_to_all | solution.py:241
  101.0 1.8 %center_grad.1 = f32[16,512]{1,0:T(8,128)} custom-call(bf16[16,512]{1,0:T(8,128)(2,1)S(1)} %copy-done.15, bf16[32,16,512]{2,1,0:T(8,128)(2,1)} %all-to-all-done.1.terms_ref), custom_call_target="tpu_custom_call" | custom-call | bytes 524288 | tf_op jit(solution)/shard_map/center_grad/pallas_call | solution.py:244
  (56 shorter events, 14.8 us)
Async XLA Ops:
  0.6 38.4 %copy-start.6 = (bf16[1024,512]{1,0:T(8,128)(2,1)S(1)}, bf16[1024,512]{1,0:T(8,128)(2,1)}, u32[]{:S(2)}) copy-start(bf16[1024,512]{1,0:T(8,128)(2,1)} %features_ref.1) | copy-start | bytes 3145732
  3.2 29.3 %all-to-all-start = ((bf16[32,16,512]{2,1,0:T(8,128)(2,1)}), bf16[32,16,512]{2,1,0:T(8,128)(2,1)S(1)}, u32[]{:S(2)}, u32[]{:S(2)}) async-start(bf16[32,16,512]{2,1,0:T(8,128)(2,1)} %broadcast_in_dim.3), calls=%async_computation | async-start | bytes 1048576 | tf_op jit(solution)/shard_map/all_to_all | solution.py:186
  14.7 24.3 %collective-permute-start.3 = (bf16[1024,512]{1,0:T(8,128)(2,1)}, bf16[1024,512]{1,0:T(8,128)(2,1)}, u32[]{:S(2)}, u32[]{:S(2)}) collective-permute-start(bf16[1024,512]{1,0:T(8,128)(2,1)} %features_ref.1), channel_id=1, source_target_pairs={{0,1},{1,0},{2,3},{3,2},{4,5},{5,4},{6,7},{7,6},{8,9},{9,8},{10,11... | collective-permute-start | bytes 3145736 | tf_op jit(solution)/shard_map/ppermute | solution.py:192
  32.5 14.1 %collective-permute-start = (bf16[512,512]{1,0:T(8,128)(2,1)S(1)}, bf16[512,512]{1,0:T(8,128)(2,1)S(1)}, u32[]{:S(2)}, u32[]{:S(2)}) collective-permute-start(bf16[512,512]{1,0:T(8,128)(2,1)S(1)} %bitcast.5), channel_id=1, source_target_pairs={{0,2},{1,9},{2,4},{3,11},{4,6},{5,13},{6,0},{7,15},{8,10},{9,17},{... | collective-permute-start | bytes 1572872 | tf_op jit(solution)/shard_map/ppermute | solution.py:190
  34.3 14.2 %collective-permute-start.2 = (bf16[512,512]{1,0:T(8,128)(2,1)S(1)}, bf16[512,512]{1,0:T(8,128)(2,1)S(1)}, u32[]{:S(2)}, u32[]{:S(2)}) collective-permute-start(bf16[512,512]{1,0:T(8,128)(2,1)S(1)} %bitcast.6), channel_id=1, source_target_pairs={{0,6},{1,25},{2,0},{3,27},{4,2},{5,29},{6,4},{7,31},{8,14},{9,1},{... | collective-permute-start | bytes 1572872 | tf_op jit(solution)/shard_map/ppermute | solution.py:190
  34.6 1.4 %collective-permute-start.4 = (s32[1024]{0:T(1024)}, s32[1024]{0:T(1024)S(1)}, u32[]{:S(2)}, u32[]{:S(2)}) collective-permute-start(s32[1024]{0:T(1024)} %param.6), channel_id=1, source_target_pairs={{0,1},{1,0},{2,3},{3,2},{4,5},{5,4},{6,7},{7,6},{8,9},{9,8},{10,11... | collective-permute-start | bytes 12296 | tf_op jit(solution)/shard_map/ppermute | solution.py:193
  34.6 17.9 %collective-permute-start.6 = (f32[1024]{0:T(1024)}, f32[1024]{0:T(1024)S(1)}, u32[]{:S(2)}, u32[]{:S(2)}) collective-permute-start(f32[1024]{0:T(1024)} %param.7), channel_id=1, source_target_pairs={{0,1},{1,0},{2,3},{3,2},{4,5},{5,4},{6,7},{7,6},{8,9},{9,8},{10,11... | collective-permute-start | bytes 12296 | tf_op jit(solution)/shard_map/ppermute | solution.py:194
  36.0 14.5 %collective-permute-start.1 = (bf16[512,512]{1,0:T(8,128)(2,1)S(1)}, bf16[512,512]{1,0:T(8,128)(2,1)S(1)}, u32[]{:S(2)}, u32[]{:S(2)}) collective-permute-start(bf16[512,512]{1,0:T(8,128)(2,1)S(1)} %bitcast.7), channel_id=1, source_target_pairs={{0,4},{1,17},{2,6},{3,19},{4,0},{5,21},{6,2},{7,23},{8,12},{9,25},... | collective-permute-start | bytes 1572872 | tf_op jit(solution)/shard_map/ppermute | solution.py:190
  48.5 3.8 %copy-start.8 = (bf16[512,512]{1,0:T(8,128)(2,1)}, bf16[512,512]{1,0:T(8,128)(2,1)S(1)}, u32[]{:S(2)}) copy-start(bf16[512,512]{1,0:T(8,128)(2,1)S(1)} %collective-permute-done.2.refs_0_.refs_3_) | copy-start | bytes 1572868
  50.4 2.0 %copy-start.16 = (f32[1024]{0:T(1024)S(1)}, f32[1024]{0:T(1024)}, u32[]{:S(2)}) copy-start(f32[1024]{0:T(1024)} %param.7) | copy-start | bytes 12292
  50.5 20.1 %copy-start.12 = (bf16[512,512]{1,0:T(8,128)(2,1)}, bf16[512,512]{1,0:T(8,128)(2,1)S(1)}, u32[]{:S(2)}) copy-start(bf16[512,512]{1,0:T(8,128)(2,1)S(1)} %collective-permute-done.1.refs_0_.refs_2_) | copy-start | bytes 1572868
  52.4 1.3 %collective-permute-start.5 = (f32[2,2048]{1,0:T(2,128)S(1)}, f32[2,2048]{1,0:T(2,128)S(1)}, u32[]{:S(2)}, u32[]{:S(2)}) collective-permute-start(f32[2,2048]{1,0:T(2,128)S(1)} %totals2.1.refs_4_), channel_id=1, source_target_pairs={{0,1},{1,0},{2,3},{3,2},{4,5},{5,4},{6,7},{7,6},{8,9},{9,8},{10,11... | collective-permute-start | bytes 49160 | tf_op jit(solution)/shard_map/ppermute | solution.py:217
  57.0 17.0 %collective-permute-start.10 = (bf16[512,512]{1,0:T(8,128)(2,1)S(1)}, bf16[512,512]{1,0:T(8,128)(2,1)S(1)}, u32[]{:S(2)}, u32[]{:S(2)}) collective-permute-start(bf16[512,512]{1,0:T(8,128)(2,1)S(1)} %get-tuple-element.21), channel_id=1, source_target_pairs={{0,2},{1,9},{2,4},{3,11},{4,6},{5,13},{6,0},{7,15},{8,10},{9,17},{... | collective-permute-start | bytes 1572872 | tf_op jit(solution)/shard_map/ppermute | solution.py:227
  62.2 8.4 %copy-start = (bf16[512,2048]{1,0:T(8,128)(2,1)}, bf16[512,2048]{1,0:T(8,128)(2,1)S(1)}, u32[]{:S(2)}) copy-start(bf16[512,2048]{1,0:T(8,128)(2,1)S(1)} %get-tuple-element.16.refs_6_) | copy-start | bytes 6291460
  62.2 11.9 %collective-permute-start.9 = (bf16[512,512]{1,0:T(8,128)(2,1)S(1)}, bf16[512,512]{1,0:T(8,128)(2,1)S(1)}, u32[]{:S(2)}, u32[]{:S(2)}) collective-permute-start(bf16[512,512]{1,0:T(8,128)(2,1)S(1)} %get-tuple-element.20), channel_id=1, source_target_pairs={{0,4},{1,17},{2,6},{3,19},{4,0},{5,21},{6,2},{7,23},{8,12},{9,25},... | collective-permute-start | bytes 1572872 | tf_op jit(solution)/shard_map/ppermute | solution.py:227
  65.4 5.2 %copy-start.2 = (bf16[512,2048]{1,0:T(8,128)(2,1)}, bf16[512,2048]{1,0:T(8,128)(2,1)S(1)}, u32[]{:S(2)}) copy-start(bf16[512,2048]{1,0:T(8,128)(2,1)S(1)} %get-tuple-element.15.refs_5_) | copy-start | bytes 6291460
  65.4 5.2 %copy-start.10 = (bf16[512,512]{1,0:T(8,128)(2,1)S(1)}, bf16[512,512]{1,0:T(8,128)(2,1)}, u32[]{:S(2)}) copy-start(bf16[512,512]{1,0:T(8,128)(2,1)} %copy-done.8) | copy-start | bytes 1572868
  65.4 13.2 %collective-permute-start.8 = (bf16[512,512]{1,0:T(8,128)(2,1)S(1)}, bf16[512,512]{1,0:T(8,128)(2,1)S(1)}, u32[]{:S(2)}, u32[]{:S(2)}) collective-permute-start(bf16[512,512]{1,0:T(8,128)(2,1)S(1)} %get-tuple-element.19), channel_id=1, source_target_pairs={{0,6},{1,25},{2,0},{3,27},{4,2},{5,29},{6,4},{7,31},{8,14},{9,1},{... | collective-permute-start | bytes 1572872 | tf_op jit(solution)/shard_map/ppermute | solution.py:227
  70.6 3.4 %copy-start.4 = (bf16[512,2048]{1,0:T(8,128)(2,1)}, bf16[512,2048]{1,0:T(8,128)(2,1)S(1)}, u32[]{:S(2)}) copy-start(bf16[512,2048]{1,0:T(8,128)(2,1)S(1)} %get-tuple-element.14.refs_4_) | copy-start | bytes 6291460
  74.0 19.8 %collective-permute-start.7 = (bf16[512,1024]{1,0:T(8,128)(2,1)}, bf16[512,1024]{1,0:T(8,128)(2,1)}, u32[]{:S(2)}, u32[]{:S(2)}) collective-permute-start(bf16[512,1024]{1,0:T(8,128)(2,1)} %rows_other.1), channel_id=1, source_target_pairs={{0,1},{1,0},{2,3},{3,2},{4,5},{5,4},{6,7},{7,6},{8,9},{9,8},{10,11... | collective-permute-start | bytes 3145736 | tf_op jit(solution)/shard_map/ppermute | solution.py:232
  79.7 21.3 %all-to-all-start.1 = ((bf16[32,16,512]{2,1,0:T(8,128)(2,1)}), bf16[32,16,512]{2,1,0:T(8,128)(2,1)}, u32[]{:S(2)}, u32[]{:S(2)}) async-start(bf16[32,16,512]{2,1,0:T(8,128)(2,1)} %bitcast.12), calls=%async_computation.1 | async-start | bytes 1048576 | tf_op jit(solution)/shard_map/all_to_all | solution.py:241
  84.6 1.6 %copy-start.1 = (bf16[512,2048]{1,0:T(8,128)(2,1)S(1)}, bf16[512,2048]{1,0:T(8,128)(2,1)}, u32[]{:S(2)}) copy-start(bf16[512,2048]{1,0:T(8,128)(2,1)} %copy-done) | copy-start | bytes 6291460
  91.4 2.4 %copy-start.7 = (bf16[1024,512]{1,0:T(8,128)(2,1)S(1)}, bf16[1024,512]{1,0:T(8,128)(2,1)}, u32[]{:S(2)}) copy-start(bf16[1024,512]{1,0:T(8,128)(2,1)} %features_ref.1) | copy-start | bytes 3145732
  93.8 7.2 %copy-start.15 = (bf16[16,512]{1,0:T(8,128)(2,1)S(1)}, bf16[16,512]{1,0:T(8,128)(2,1)}, u32[]{:S(2)}) copy-start(bf16[16,512]{1,0:T(8,128)(2,1)} %centers_ref.1) | copy-start | bytes 49156
  (6 other events, 7.2 us)
